TPU v7x, 512 devices: a whole 4x4x16 slice. The times are simulated.
512 devices in a mesh: row: 32 (over x, y, core), col: 16 (over z).
Axes of the slice: x: 4, y: 4, z: 16, core: 2. Of those that a mesh axis runs over, the one named last changes fastest.
Arguments:
- diag_factor: float32 [1024, 1024], P('row', 'col'), may hold values from -1 to 2.5, as said below
- panel_factor: float32 [16384, 1024], P('row', 'col'), may hold values from -0.046875 to 0.046875
- left_factor: float32 [16384, 8192], P('row', 'col'), may hold values from -0.046875 to 0.046875
- pivot_factor: float32 [1024, 8192], P('row', 'col'), may hold values from -0.1875 to 0.1875
- panel_adjoint: float32 [16384, 1024], P('row', 'col'), may hold values from -6 to 6
- left_adjoint: float32 [16384, 8192], P('row', 'col'), may hold values from -6 to 6
- pivot_adjoint: float32 [1024, 8192], P('row', 'col'), may hold values from -6 to 6
- diag_adjoint: float32 [1024, 1024], P('row', 'col'), may hold values from -6 to 6
Outputs:
- solved_panel: float32 [16384, 1024], P('row', 'col')
- left_out: float32 [16384, 8192], P('row', 'col')
- pivot_out: float32 [1024, 8192], P('row', 'col')
- diag_out: float32 [1024, 1024], P('row', 'col')
Inputs may be any that keep to these rules, and one draw needn't show every extreme that they name: diag_factor is lower triangular: zero above the diagonal, diagonal entries at least 1.
All inputs are finite; a program needn't handle non-finite values.
Results may differ from a plain program's by a relative error of at most 0.000073.
Values sent between devices are 32-bit elements; how exact they have to be, the bound alone decides.
A program may use at most 64 MiB of HBM per device.

v0:
```python
import jax
import jax.numpy as jnp
from jax import lax
from jax.sharding import PartitionSpec as P


def right_solve(tile, source):
    return jax.scipy.linalg.solve_triangular(tile, source.T, trans="T", lower=True).T


def local(
    diag_factor,
    panel_factor,
    left_factor,
    pivot_factor,
    panel_adjoint,
    left_adjoint,
    pivot_adjoint,
    diag_adjoint,
):
    highest = lax.Precision.HIGHEST
    block_width = panel_adjoint.shape[1]
    my_col = lax.axis_index("col")
    my_row = lax.axis_index("row")
    column_block = lax.all_gather(diag_factor, "row", axis=0, tiled=True)
    whole_diag = lax.all_gather(column_block, "col", axis=1, tiled=True)
    full_rows = lax.all_gather(panel_adjoint, "col", axis=1, tiled=True)
    solved = right_solve(whole_diag, full_rows)
    solved_panel = lax.dynamic_slice_in_dim(solved, my_col * block_width, block_width, 1)
    picked = solved
    left_out = left_adjoint - jnp.dot(
        picked,
        lax.all_gather(pivot_factor, "row", axis=0, tiled=True),
        precision=highest,
        preferred_element_type=jnp.float32,
    )
    own_rows = diag_adjoint.shape[0]
    picked = solved
    pivot_sum = lax.psum_scatter(
        jnp.einsum("rk,rc->kc", picked, left_factor, precision=highest),
        "row",
        scatter_dimension=0,
        tiled=True,
    )
    picked = solved
    square_sum = lax.psum_scatter(
        jnp.einsum("rk,rc->kc", picked, panel_factor, precision=highest),
        "row",
        scatter_dimension=0,
        tiled=True,
    )
    pivot_out = pivot_adjoint - pivot_sum
    global_row = my_row * own_rows + lax.broadcasted_iota(jnp.int32, (own_rows, block_width), 0)
    global_col = my_col * block_width + lax.broadcasted_iota(jnp.int32, (own_rows, block_width), 1)
    diag_out = diag_adjoint - jnp.where(global_col <= global_row, square_sum, 0.0)
    return (solved_panel, left_out, pivot_out, diag_out)


def solution(mesh):
    in_specs = (
        P("row", "col"),
        P("row", "col"),
        P("row", "col"),
        P("row", "col"),
        P("row", "col"),
        P("row", "col"),
        P("row", "col"),
        P("row", "col"),
    )
    out_specs = (P("row", "col"), P("row", "col"), P("row", "col"), P("row", "col"))
    return jax.shard_map(local, mesh=mesh, in_specs=in_specs, out_specs=out_specs, check_vma=False)
```

profile of v0, /device:TPU:2, one launch (start us, length us, event | category | flops | bytes accessed | tf_op | source)
XLA Modules:
  0.0 463.6 jit_solution(8965409141635587499)
XLA Ops:
  7.2 27.8 %all_gather.12 = f32[1024,64]{1,0:T(8,128)S(1)} all-gather(f32[32,64]{1,0:T(8,128)} %param.8), channel_id=1, replica_groups=mesh['row'=32,'col'=16] {'row'}, dimensions={0}, use_global_device_ids=true | all-gather | bytes 270336 | tf_op jit(solution)/shard_map/all_gather | solution.py:25
  35.0 0.9 copy.14
  36.0 0.7 all-gather.6.cloned.1.call-update
  36.7 0.7 all-gather.8.cloned.1.call-update
  37.5 77.2 %all-gather.4.cloned.1.call-done = f32[1024,1024]{0,1:T(8,128)} async-done(((f32[1024,64]{0,1:T(8,128)}), f32[1024,1024]{0,1:T(8,128)}) %all-gather.4.cloned.1.call-update) | async-done | bytes 4194320 | tf_op jit(solution)/shard_map/all_gather | solution.py:26
  114.7 4.8 %fusion = f32[1024,1024]{0,1:T(8,128)} fusion(f32[1024,1024]{0,1:T(8,128)} %all-gather.4.cloned.1.call-done), kind=kLoop, calls=%fused_computation.3 | loop fusion | flops 2097152 | bytes 8388608 | tf_op jit(solution)/shard_map/jit(_solve_triangular)/triangular_solve | solution.py:8
  119.5 24.1 %while.1 = (s32[]{:T(128)}, f32[1024,1024]{0,1:T(8,128)}, s32[8,2]{0,1:T(2,128)S(1)}, f32[8,128,128]{2,1,0:T(8,128)S(1)}, s32[]{:T(128)}) while((s32[]{:T(128)}, f32[1024,1024]{0,1:T(8,128)}, s32[8,2]{0,1:T(2,128)S(1)}, f32[8,128,128]{2,1,0:T(8,128)S(1)}, s32[]{:T(128)}) %tuple.28), condition=%wide.while_cond, body=%wide.while_body.sunk | while | flops 2 | bytes 393321 | solution.py:8
  119.5 0.1 constant_dynamic-slice_fusion.2
  119.5 0.5 fusion.55
  120.1 2.3 dynamic-slice.12
  122.4 0.1 copy.18
  122.5 0.1 constant_dynamic-slice_fusion.2
  122.6 0.5 fusion.55
  123.1 2.3 dynamic-slice.12
  125.4 0.1 copy.18
  125.5 0.1 constant_dynamic-slice_fusion.2
  125.6 0.5 fusion.55
  126.1 2.3 dynamic-slice.12
  128.4 0.1 copy.18
  128.5 0.1 constant_dynamic-slice_fusion.2
  128.6 0.5 fusion.55
  129.1 2.3 dynamic-slice.12
  131.4 0.1 copy.18
  131.6 0.1 constant_dynamic-slice_fusion.2
  131.6 0.5 fusion.55
  132.2 2.3 dynamic-slice.12
  134.5 0.1 copy.18
  134.6 0.1 constant_dynamic-slice_fusion.2
  134.7 0.5 fusion.55
  135.2 2.3 dynamic-slice.12
  137.5 0.1 copy.18
  137.6 0.1 constant_dynamic-slice_fusion.2
  137.7 0.5 fusion.55
  138.2 2.3 dynamic-slice.12
  140.5 0.1 copy.18
  140.6 0.1 constant_dynamic-slice_fusion.2
  140.7 0.5 fusion.55
  141.2 2.2 dynamic-slice.12
  143.5 0.1 copy.18
  143.6 78.6 %custom-call.4 = f32[8,128,128]{1,2,0:T(8,128)S(1)} custom-call(f32[8,128,128]{2,1,0:T(8,128)S(1)} %get-tuple-element.11), custom_call_target="InvertDiagBlocksLowerTriangular" | custom-call | tf_op jit(solution)/shard_map/jit(_solve_triangular)/triangular_solve | solution.py:8
  222.2 1.5 fusion.19
  223.8 1.4 convolution_subtract_fusion.4
  225.1 0.4 fusion.25
  225.5 1.4 convolution_subtract_fusion.3
  227.0 0.4 fusion.26
  227.3 1.6 convolution_subtract_fusion.6
  228.9 0.4 fusion.27
  229.3 1.7 convolution_subtract_fusion.7
  230.9 0.4 constant_dynamic-update-slice_fusion.4
  231.4 1.9 convolution_subtract_fusion.2
  233.3 0.4 constant_dynamic-update-slice_fusion.10
  233.8 2.0 convolution_subtract_fusion.5
  235.9 0.4 constant_dynamic-update-slice_fusion.17
  236.4 2.2 convolution_subtract_fusion.1
  238.6 1.2 convolution_dynamic-update-slice_fusion
  240.1 2.6 fusion.36
  242.7 0.3 reduce-scatter.3.cloned.1.call-start
  243.0 4.8 %fusion.35 = f32[1024,512]{1,0:T(8,128)} fusion(f32[1024,512]{1,0:T(8,128)S(1)} %constant_dynamic-update-slice_fusion.18, f32[512,512]{1,0:T(8,128)S(1)} %copy-done), kind=kOutput, calls=%fused_computation.85 | convolution fusion | flops 3221225472 | bytes 5242880 | tf_op jit(solution)/shard_map/rk,rc->kc/dot_general | solution.py:40
  247.8 0.7 dynamic-slice_bitcast_fusion
  248.5 6.3 %convolution_subtract_fusion = f32[512,512]{1,0:T(8,128)} fusion(f32[512,512]{1,0:T(8,128)} %param.13, f32[1024,512]{1,0:T(8,128)S(1)} %constant_dynamic-update-slice_fusion.18, f32[1024,512]{1,0:T(8,128)} %all-gather.8.cloned.1.call-done), kind=kOutput, calls=%fused_computation.4 | convolution fusion | flops 3221487616 | bytes 6291456 | tf_op jit(solution)/shard_map/dot_general | solution.py:31
  254.9 95.1 %reduce-scatter.5.cloned.1.call-done = f32[32,64]{1,0:T(8,128)} async-done(((f32[1024,64]{1,0:T(8,128)}), f32[32,64]{1,0:T(8,128)}) %reduce-scatter.5.cloned.1.call-update) | async-done | bytes 8208 | tf_op jit(solution)/shard_map/reduce_scatter | solution.py:46
  349.9 1.4 select_subtract_fusion
  351.3 104.3 %reduce-scatter.3.cloned.1.call-done = f32[32,512]{1,0:T(8,128)} async-done(((f32[1024,512]{1,0:T(8,128)}), f32[32,512]{1,0:T(8,128)}) %reduce-scatter.3.cloned.1.call-update) | async-done | bytes 65552 | tf_op jit(solution)/shard_map/reduce_scatter | solution.py:39
  455.6 1.5 sub.10
  (56 shorter events, 0.8 us)
Async XLA Ops:
  7.2 235.8 %copy-start = (f32[512,512]{1,0:T(8,128)S(1)}, f32[512,512]{1,0:T(8,128)}, u32[]{:S(2)}) copy-start(f32[512,512]{1,0:T(8,128)} %param.10) | copy-start | bytes 3145732
  7.2 107.5 %all-gather.4.cloned.1.call-start = ((), (), s32[]{:S(2)}) async-start(), calls=%async_computation.2 | async-start | bytes 4456448 | tf_op jit(solution)/shard_map/all_gather | solution.py:26
  35.9 186.3 %all-gather.6.cloned.1.call-start = ((), (), s32[]{:S(2)}) async-start(), calls=%async_computation.3 | async-start | bytes 2228224 | tf_op jit(solution)/shard_map/all_gather | solution.py:27
  36.7 211.8 %all-gather.8.cloned.1.call-start = ((), (), s32[]{:S(2)}) async-start(), calls=%async_computation.4 | async-start | bytes 2162688 | tf_op jit(solution)/shard_map/all_gather | solution.py:33
  37.4 312.5 %reduce-scatter.5.cloned.1.call-start = ((), (), s32[]{:S(2)}) async-start(), calls=%async_computation.6 | async-start | bytes 540672 | tf_op jit(solution)/shard_map/reduce_scatter | solution.py:46
  222.2 13.7 %copy-start.2 = (f32[8,128,128]{1,2,0:T(8,128)}, f32[8,128,128]{1,2,0:T(8,128)S(1)}, u32[]{:S(2)}) copy-start(f32[8,128,128]{1,2,0:T(8,128)S(1)} %custom-call.4) | copy-start | bytes 1572868
  222.2 5.1 %copy-start.1 = (f32[512,1024]{0,1:T(8,128)S(1)}, f32[512,1024]{0,1:T(8,128)}, u32[]{:S(2)}) copy-start(f32[512,1024]{0,1:T(8,128)} %all-gather.6.cloned.1.call-done) | copy-start | bytes 6291460
  238.6 1.5 copy-start.3
  242.7 212.9 %reduce-scatter.3.cloned.1.call-start = ((), (), s32[]{:S(2)}) async-start(), calls=%async_computation.5 | async-start | bytes 2162688 | tf_op jit(solution)/shard_map/reduce_scatter | solution.py:39
  248.5 101.4 %copy-start.5 = (f32[32,64]{1,0:T(8,128)S(1)}, f32[32,64]{1,0:T(8,128)}, u32[]{:S(2)}) copy-start(f32[32,64]{1,0:T(8,128)} %param.15) | copy-start | bytes 24580
  248.5 207.1 %copy-start.4 = (f32[32,512]{1,0:T(8,128)S(1)}, f32[32,512]{1,0:T(8,128)}, u32[]{:S(2)}) copy-start(f32[32,512]{1,0:T(8,128)} %param.14) | copy-start | bytes 196612
Sparse Core Ops, SparseCore 0:
  36.0 78.6 all-gather.3
  116.8 70.5 all-gather.5
  190.5 55.6 all-gather.7
  250.3 99.5 reduce-scatter.4
  354.2 101.3 reduce-scatter.2
where the time goes:
time: 465 us; the launch traced here: 464 us
  waiting for transfers between devices  278 us (60%)
  other arithmetic  86.2 us (19%)
  matrix products  30.8 us (7%)
  blocking collectives  27.8 us (6%)
  local copies, waits for them, and re-layouts  25.9 us (6%)
  between operations  14.2 us (3%)
    reduce_scatter x1, waiting for transfers between devices, local(): lax.psum_scatter(jnp.einsum('rk,rc->kc', picked, left_factor, precision=h...  104 us
    reduce_scatter x1, waiting for transfers between devices, local(): lax.psum_scatter(jnp.einsum('rk,rc->kc', picked, panel_factor, precision=...  95.1 us
    another operation x3, other arithmetic, right_solve(): jax.scipy.linalg.solve_triangular(tile, source.T, trans='T', lower=True)  83.4 us
    all_gather x1, waiting for transfers between devices, local(): whole_diag = lax.all_gather(column_block, 'col', axis=1, tiled=True)  77.2 us
    all_gather x1, blocking collectives, local(): column_block = lax.all_gather(diag_factor, 'row', axis=0, tiled=True)  27.8 us
    another operation x40, local copies, waits for them, and re-layouts  23.8 us
    another operation x15, matrix products, right_solve(): jax.scipy.linalg.solve_triangular(tile, source.T, trans='T', lower=True)  17.1 us
  transfers between devices with their start and end apart: 5, of which 3 were waited for; matrix products, arithmetic and copies ran while one was open for 30% of the time, Pallas kernels for 0%

commit v1 on v0

--- a/solution.py
+++ b/solution.py
@@ -2,6 +2,28 @@
 import jax.numpy as jnp
 from jax import lax
 from jax.sharding import PartitionSpec as P
+
+
+def joined_along(pieces, dim):
+    lengths = list(pieces.shape[1:])
+    lengths[dim] *= pieces.shape[0]
+    return jnp.moveaxis(pieces, 0, dim).reshape(lengths)
+
+
+def collect(x, axis, dim):
+    peers = lax.axis_size(axis)
+    pairs = [(i, (i + 1) % peers) for i in range(peers)]
+    back = [(b, a) for a, b in pairs]
+    lower, upper = ([], [])
+    for step in range(peers - 1):
+        if step % 2 == 0:
+            lower.append(lax.ppermute(lower[-1] if lower else x, axis, pairs))
+        else:
+            upper.append(lax.ppermute(upper[-1] if upper else x, axis, back))
+    tiles = jnp.stack([*lower[::-1], x, *upper])
+    shift = lax.axis_index(axis) - len(lower)
+    tiles = tiles[(jnp.arange(peers) - shift) % peers]
+    return joined_along(tiles, dim)
 
 
 def right_solve(tile, source):
@@ -23,7 +45,7 @@
     my_col = lax.axis_index("col")
     my_row = lax.axis_index("row")
     column_block = lax.all_gather(diag_factor, "row", axis=0, tiled=True)
-    whole_diag = lax.all_gather(column_block, "col", axis=1, tiled=True)
+    whole_diag = collect(column_block, "col", 1)
     full_rows = lax.all_gather(panel_adjoint, "col", axis=1, tiled=True)
     solved = right_solve(whole_diag, full_rows)
     solved_panel = lax.dynamic_slice_in_dim(solved, my_col * block_width, block_width, 1)

time: 465 us -> 502 us (1.080)
  starting transfers between devices: 0.42 us -> 51.6 us
  waiting for transfers between devices: 278 us -> 236 us
  local copies, waits for them, and re-layouts: 25.9 us -> 52.5 us
    all_gather x1 -> x0, waiting for transfers between devices: 77.2 us -> none  [local(): whole_diag = lax.all_gather(column_block, 'col', axis=1, tiled=True)]
    ppermute x0 -> x15, starting transfers between devices: none -> 51.2 us  [the longest x7 35.9 us: collect(): upper.append(lax.ppermute(upper[-1] if upper else x, axis, back))]
    ppermute x0 -> x15, waiting for transfers between devices: none -> 44.5 us  [the longest x8 44.5 us: collect(): lower.append(lax.ppermute(lower[-1] if lower else x, axis, pairs))]
    unnamed x30 -> x47, local copies, waits for them, and re-layouts: 0.39 us -> 17 us
    reduce_scatter x1, waiting for transfers between devices: 95.1 us -> 86.8 us  [local(): lax.psum_scatter(jnp.einsum('rk,rc->kc', picked, panel_factor, precision=...]
    another operation x40 -> x41, local copies, waits for them, and re-layouts: 23.8 us -> 29.6 us
    gather x0 -> x1, local copies, waits for them, and re-layouts: none -> 5.03 us  [collect(): tiles = tiles[(jnp.arange(peers) - shift) % peers]]
  transfers between devices with their start and end apart: 5 -> 19, of which waited for: 3 -> 10; matrix products, arithmetic and copies ran while one was open for 30% -> 34% of each run, Pallas kernels for 0% -> 0%
where the time goes in v1:
time: 502 us; the launch traced here: 500 us
  waiting for transfers between devices  236 us (47%)
  other arithmetic  87 us (17%)
  local copies, waits for them, and re-layouts  52.5 us (10%)
  starting transfers between devices  51.6 us (10%)
  matrix products  30.8 us (6%)
  blocking collectives  27.6 us (5%)
  between operations  14.4 us (3%)
    reduce_scatter x1, waiting for transfers between devices, local(): lax.psum_scatter(jnp.einsum('rk,rc->kc', picked, left_factor, precision=h...  104 us
    reduce_scatter x1, waiting for transfers between devices, local(): lax.psum_scatter(jnp.einsum('rk,rc->kc', picked, panel_factor, precision=...  86.8 us
    another operation x3, other arithmetic, right_solve(): jax.scipy.linalg.solve_triangular(tile, source.T, trans='T', lower=True)  84.1 us
    ppermute x8, waiting for transfers between devices, collect(): lower.append(lax.ppermute(lower[-1] if lower else x, axis, pairs))  44.5 us
    ppermute x7, starting transfers between devices, collect(): upper.append(lax.ppermute(upper[-1] if upper else x, axis, back))  35.9 us
    another operation x40, local copies, waits for them, and re-layouts  28.9 us
    all_gather x1, blocking collectives, local(): column_block = lax.all_gather(diag_factor, 'row', axis=0, tiled=True)  27.6 us
    another operation x15, matrix products, right_solve(): jax.scipy.linalg.solve_triangular(tile, source.T, trans='T', lower=True)  17.1 us
  transfers between devices with their start and end apart: 19, of which 10 were waited for; matrix products, arithmetic and copies ran while one was open for 34% of the time, Pallas kernels for 0%

profile of v1, /device:TPU:2, one launch (start us, length us, event | category | flops | bytes accessed | tf_op | source)
XLA Modules:
  0.0 500.4 jit_solution(3875449213080011782)
XLA Ops:
  8.0 27.6 %all_gather.9 = f32[1024,64]{1,0:T(8,128)S(1)} all-gather(f32[32,64]{1,0:T(8,128)} %param.8), channel_id=1, replica_groups=mesh['row'=32,'col'=16] {'row'}, dimensions={0}, use_global_device_ids=true | all-gather | bytes 270336 | tf_op jit(solution)/shard_map/all_gather | solution.py:47
  35.8 1.9 collective-permute-start
  37.7 16.2 %collective-permute-done = f32[1024,64]{0,1:T(8,128)S(1)} collective-permute-done((f32[1024,64]{0,1:T(8,128)S(1)}, f32[1024,64]{0,1:T(8,128)S(1)}, u32[]{:S(2)}, u32[]{:S(2)}) %collective-permute-start) | collective-permute-done | bytes 262176 | tf_op jit(solution)/shard_map/ppermute | solution.py:20
  54.0 1.9 collective-permute-start.1
  55.9 5.1 %collective-permute-start.8 = (f32[1024,64]{0,1:T(8,128)S(1)}, f32[1024,64]{0,1:T(8,128)S(1)}, u32[]{:S(2)}, u32[]{:S(2)}) collective-permute-start(f32[1024,64]{0,1:T(8,128)S(1)} %copy.16), channel_id=1, source_target_pairs={{1,0},{2,1},{3,2},{4,3},{5,4},{6,5},{7,6},{8,7},{9,8},{10,9},{11,1... | collective-permute-start | bytes 786440 | tf_op jit(solution)/shard_map/ppermute | solution.py:22
  61.0 8.1 %collective-permute-done.1 = f32[1024,64]{0,1:T(8,128)S(1)} collective-permute-done((f32[1024,64]{0,1:T(8,128)S(1)}, f32[1024,64]{0,1:T(8,128)S(1)}, u32[]{:S(2)}, u32[]{:S(2)}) %collective-permute-start.1) | collective-permute-done | bytes 262176 | tf_op jit(solution)/shard_map/ppermute | solution.py:20
  69.2 1.9 collective-permute-start.2
  71.1 5.1 %collective-permute-start.9 = (f32[1024,64]{0,1:T(8,128)S(1)}, f32[1024,64]{0,1:T(8,128)S(1)}, u32[]{:S(2)}, u32[]{:S(2)}) collective-permute-start(f32[1024,64]{0,1:T(8,128)S(1)} %collective-permute-done.8), channel_id=1, source_target_pairs={{1,0},{2,1},{3,2},{4,3},{5,4},{6,5},{7,6},{8,7},{9,8},{10,9},{11,1... | collective-permute-start | bytes 786440 | tf_op jit(solution)/shard_map/ppermute | solution.py:22
  76.2 6.5 %collective-permute-done.2 = f32[1024,64]{0,1:T(8,128)S(1)} collective-permute-done((f32[1024,64]{0,1:T(8,128)S(1)}, f32[1024,64]{0,1:T(8,128)S(1)}, u32[]{:S(2)}, u32[]{:S(2)}) %collective-permute-start.2) | collective-permute-done | bytes 262176 | tf_op jit(solution)/shard_map/ppermute | solution.py:20
  82.7 1.9 collective-permute-start.3
  84.6 5.1 %collective-permute-start.10 = (f32[1024,64]{0,1:T(8,128)S(1)}, f32[1024,64]{0,1:T(8,128)S(1)}, u32[]{:S(2)}, u32[]{:S(2)}) collective-permute-start(f32[1024,64]{0,1:T(8,128)S(1)} %collective-permute-done.9), channel_id=1, source_target_pairs={{1,0},{2,1},{3,2},{4,3},{5,4},{6,5},{7,6},{8,7},{9,8},{10,9},{11,1... | collective-permute-start | bytes 786440 | tf_op jit(solution)/shard_map/ppermute | solution.py:22
  89.8 3.4 collective-permute-done.3
  93.2 1.9 collective-permute-start.4
  95.1 5.1 %collective-permute-start.11 = (f32[1024,64]{0,1:T(8,128)S(1)}, f32[1024,64]{0,1:T(8,128)S(1)}, u32[]{:S(2)}, u32[]{:S(2)}) collective-permute-start(f32[1024,64]{0,1:T(8,128)S(1)} %collective-permute-done.10), channel_id=1, source_target_pairs={{1,0},{2,1},{3,2},{4,3},{5,4},{6,5},{7,6},{8,7},{9,8},{10,9},{11,1... | collective-permute-start | bytes 786440 | tf_op jit(solution)/shard_map/ppermute | solution.py:22
  100.3 2.4 collective-permute-done.4
  102.7 1.9 collective-permute-start.5
  104.6 5.1 %collective-permute-start.12 = (f32[1024,64]{0,1:T(8,128)S(1)}, f32[1024,64]{0,1:T(8,128)}, u32[]{:S(2)}, u32[]{:S(2)}) collective-permute-start(f32[1024,64]{0,1:T(8,128)S(1)} %collective-permute-done.11), channel_id=1, source_target_pairs={{1,0},{2,1},{3,2},{4,3},{5,4},{6,5},{7,6},{8,7},{9,8},{10,9},{11,1... | collective-permute-start | bytes 786440 | tf_op jit(solution)/shard_map/ppermute | solution.py:22
  109.8 2.5 collective-permute-done.5
  112.2 1.9 collective-permute-start.6
  114.3 5.1 %collective-permute-start.13 = (f32[1024,64]{0,1:T(8,128)}, f32[1024,64]{0,1:T(8,128)}, u32[]{:S(2)}, u32[]{:S(2)}) collective-permute-start(f32[1024,64]{0,1:T(8,128)} %collective-permute-done.12), channel_id=1, source_target_pairs={{1,0},{2,1},{3,2},{4,3},{5,4},{6,5},{7,6},{8,7},{9,8},{10,9},{11,1... | collective-permute-start | bytes 786440 | tf_op jit(solution)/shard_map/ppermute | solution.py:22
  119.4 2.6 collective-permute-done.6
  122.0 1.9 collective-permute-start.7
  124.0 5.1 %collective-permute-start.14 = (f32[1024,64]{0,1:T(8,128)}, f32[1024,64]{0,1:T(8,128)S(1)}, u32[]{:S(2)}, u32[]{:S(2)}) collective-permute-start(f32[1024,64]{0,1:T(8,128)} %collective-permute-done.13), channel_id=1, source_target_pairs={{1,0},{2,1},{3,2},{4,3},{5,4},{6,5},{7,6},{8,7},{9,8},{10,9},{11,1... | collective-permute-start | bytes 786440 | tf_op jit(solution)/shard_map/ppermute | solution.py:22
  129.2 2.6 collective-permute-done.7
  131.8 1.7 bitcast_dynamic-update-slice_fusion.16
  133.5 1.7 bitcast_dynamic-update-slice_fusion.15
  135.1 1.7 bitcast_dynamic-update-slice_fusion.14
  136.8 1.7 bitcast_dynamic-update-slice_fusion.13
  139.2 0.7 bitcast_dynamic-update-slice_fusion.11
  139.9 0.8 bitcast_dynamic-update-slice_fusion.10
  140.7 0.7 bitcast_dynamic-update-slice_fusion.9
  141.4 0.7 bitcast_dynamic-update-slice_fusion.8
  142.2 0.7 bitcast_dynamic-update-slice_fusion.7
  145.0 1.7 bitcast_dynamic-update-slice_fusion.3
  146.7 1.7 bitcast_dynamic-update-slice_fusion.2
  148.4 0.7 bitcast_dynamic-update-slice_fusion.1
  149.1 5.0 %gather_fusion = f32[16,1024,64]{1,2,0:T(8,128)} fusion(f32[16,1024,64]{1,2,0:T(8,128)} %bitcast_dynamic-update-slice_fusion.1, s32[1024]{0:T(1024)S(1)} %pad_clamp_fusion), kind=kCustom, calls=%fused_computation | custom fusion | bytes 8388672 | tf_op jit(solution)/shard_map/gather | solution.py:25
  154.1 4.7 bitcast_select_fusion
  158.9 29.0 %while.1 = (s32[]{:T(128)}, f32[1024,1024]{0,1:T(8,128)}, s32[8,2]{0,1:T(2,128)S(1)}, f32[8,128,128]{2,1,0:T(8,128)}, s32[]{:T(128)}) while((s32[]{:T(128)}, f32[1024,1024]{0,1:T(8,128)}, s32[8,2]{0,1:T(2,128)S(1)}, f32[8,128,128]{2,1,0:T(8,128)}, s32[]{:T(128)}) %tuple.29), condition=%wide.while_cond, body=%wide.while_body.sunk | while | flops 2 | bytes 393829 | solution.py:30
  159.5 2.3 dynamic-slice.12
  163.1 2.3 dynamic-slice.12
  166.7 2.3 dynamic-slice.12
  170.4 2.3 dynamic-slice.12
  174.0 2.3 dynamic-slice.12
  177.6 2.3 dynamic-slice.12
  181.2 2.3 dynamic-slice.12
  184.9 2.2 dynamic-slice.12
  187.8 79.4 %custom-call.4 = f32[8,128,128]{1,2,0:T(8,128)S(1)} custom-call(f32[8,128,128]{2,1,0:T(8,128)} %get-tuple-element.11), custom_call_target="InvertDiagBlocksLowerTriangular" | custom-call | tf_op jit(solution)/shard_map/jit(_solve_triangular)/triangular_solve | solution.py:30
  267.3 1.5 fusion.18
  268.8 1.4 convolution_subtract_fusion.4
  270.6 1.4 convolution_subtract_fusion.3
  272.4 1.6 convolution_subtract_fusion.6
  274.3 1.7 convolution_subtract_fusion.7
  276.5 1.9 convolution_subtract_fusion.2
  278.9 2.0 convolution_subtract_fusion.5
  281.5 2.2 convolution_subtract_fusion.1
  283.7 1.2 convolution_dynamic-update-slice_fusion
  285.2 2.6 fusion.37
  288.0 4.8 fusion.36
  293.6 6.4 %convolution_subtract_fusion = f32[512,512]{1,0:T(8,128)} fusion(f32[512,512]{1,0:T(8,128)} %param.13, f32[1024,512]{1,0:T(8,128)S(1)} %constant_dynamic-update-slice_fusion.18, f32[1024,512]{1,0:T(8,128)} %all-gather.5.cloned.1.call-done), kind=kOutput, calls=%fused_computation.5 | convolution fusion | flops 3221487616 | bytes 6291456 | tf_op jit(solution)/shard_map/dot_general | solution.py:53
  299.9 86.8 %reduce-scatter.5.cloned.1.call-done = f32[32,64]{1,0:T(8,128)} async-done(((f32[1024,64]{1,0:T(8,128)}), f32[32,64]{1,0:T(8,128)}) %reduce-scatter.5.cloned.1.call-update) | async-done | bytes 8208 | tf_op jit(solution)/shard_map/reduce_scatter | solution.py:68
  386.7 1.4 select_subtract_fusion
  388.1 104.3 %reduce-scatter.3.cloned.1.call-done = f32[32,512]{1,0:T(8,128)} async-done(((f32[1024,512]{1,0:T(8,128)}), f32[32,512]{1,0:T(8,128)}) %reduce-scatter.3.cloned.1.call-update) | async-done | bytes 65552 | tf_op jit(solution)/shard_map/reduce_scatter | solution.py:61
  492.4 1.5 sub.29
  (104 shorter events, 18.1 us)
Async XLA Ops:
  7.2 280.9 %copy-start = (f32[512,512]{1,0:T(8,128)S(1)}, f32[512,512]{1,0:T(8,128)}, u32[]{:S(2)}) copy-start(f32[512,512]{1,0:T(8,128)} %param.10) | copy-start | bytes 3145732
  7.2 260.1 %all-gather.3.cloned.1.call-start = ((), (), s32[]{:S(2)}) async-start(), calls=%async_computation.2 | async-start | bytes 2228224 | tf_op jit(solution)/shard_map/all_gather | solution.py:49
  7.9 285.7 %all-gather.5.cloned.1.call-start = ((), (), s32[]{:S(2)}) async-start(), calls=%async_computation.3 | async-start | bytes 2162688 | tf_op jit(solution)/shard_map/all_gather | solution.py:55
  35.8 18.2 %collective-permute-start = (f32[1024,64]{0,1:T(8,128)S(1)}, f32[1024,64]{0,1:T(8,128)S(1)}, u32[]{:S(2)}, u32[]{:S(2)}) collective-permute-start(f32[1024,64]{0,1:T(8,128)S(1)} %copy.16), channel_id=1, source_target_pairs={{0,1},{1,2},{2,3},{3,4},{4,5},{5,6},{6,7},{7,8},{8,9},{9,10},{10,1... | collective-permute-start | bytes 786440 | tf_op jit(solution)/shard_map/ppermute | solution.py:20
  54.0 15.2 %collective-permute-start.1 = (f32[1024,64]{0,1:T(8,128)S(1)}, f32[1024,64]{0,1:T(8,128)S(1)}, u32[]{:S(2)}, u32[]{:S(2)}) collective-permute-start(f32[1024,64]{0,1:T(8,128)S(1)} %collective-permute-done), channel_id=1, source_target_pairs={{0,1},{1,2},{2,3},{3,4},{4,5},{5,6},{6,7},{7,8},{8,9},{9,10},{10,1... | collective-permute-start | bytes 786440 | tf_op jit(solution)/shard_map/ppermute | solution.py:20
  55.9 15.2 %collective-permute-start.8 = (f32[1024,64]{0,1:T(8,128)S(1)}, f32[1024,64]{0,1:T(8,128)S(1)}, u32[]{:S(2)}, u32[]{:S(2)}) collective-permute-start(f32[1024,64]{0,1:T(8,128)S(1)} %copy.16), channel_id=1, source_target_pairs={{1,0},{2,1},{3,2},{4,3},{5,4},{6,5},{7,6},{8,7},{9,8},{10,9},{11,1... | collective-permute-start | bytes 786440 | tf_op jit(solution)/shard_map/ppermute | solution.py:22
  69.2 13.6 %collective-permute-start.2 = (f32[1024,64]{0,1:T(8,128)S(1)}, f32[1024,64]{0,1:T(8,128)S(1)}, u32[]{:S(2)}, u32[]{:S(2)}) collective-permute-start(f32[1024,64]{0,1:T(8,128)S(1)} %collective-permute-done.1), channel_id=1, source_target_pairs={{0,1},{1,2},{2,3},{3,4},{4,5},{5,6},{6,7},{7,8},{8,9},{9,10},{10,1... | collective-permute-start | bytes 786440 | tf_op jit(solution)/shard_map/ppermute | solution.py:20
  71.1 13.6 %collective-permute-start.9 = (f32[1024,64]{0,1:T(8,128)S(1)}, f32[1024,64]{0,1:T(8,128)S(1)}, u32[]{:S(2)}, u32[]{:S(2)}) collective-permute-start(f32[1024,64]{0,1:T(8,128)S(1)} %collective-permute-done.8), channel_id=1, source_target_pairs={{1,0},{2,1},{3,2},{4,3},{5,4},{6,5},{7,6},{8,7},{9,8},{10,9},{11,1... | collective-permute-start | bytes 786440 | tf_op jit(solution)/shard_map/ppermute | solution.py:22
  82.7 10.5 %collective-permute-start.3 = (f32[1024,64]{0,1:T(8,128)S(1)}, f32[1024,64]{0,1:T(8,128)S(1)}, u32[]{:S(2)}, u32[]{:S(2)}) collective-permute-start(f32[1024,64]{0,1:T(8,128)S(1)} %collective-permute-done.2), channel_id=1, source_target_pairs={{0,1},{1,2},{2,3},{3,4},{4,5},{5,6},{6,7},{7,8},{8,9},{9,10},{10,1... | collective-permute-start | bytes 786440 | tf_op jit(solution)/shard_map/ppermute | solution.py:20
  84.6 10.5 %collective-permute-start.10 = (f32[1024,64]{0,1:T(8,128)S(1)}, f32[1024,64]{0,1:T(8,128)S(1)}, u32[]{:S(2)}, u32[]{:S(2)}) collective-permute-start(f32[1024,64]{0,1:T(8,128)S(1)} %collective-permute-done.9), channel_id=1, source_target_pairs={{1,0},{2,1},{3,2},{4,3},{5,4},{6,5},{7,6},{8,7},{9,8},{10,9},{11,1... | collective-permute-start | bytes 786440 | tf_op jit(solution)/shard_map/ppermute | solution.py:22
  93.2 9.5 %collective-permute-start.4 = (f32[1024,64]{0,1:T(8,128)S(1)}, f32[1024,64]{0,1:T(8,128)S(1)}, u32[]{:S(2)}, u32[]{:S(2)}) collective-permute-start(f32[1024,64]{0,1:T(8,128)S(1)} %collective-permute-done.3), channel_id=1, source_target_pairs={{0,1},{1,2},{2,3},{3,4},{4,5},{5,6},{6,7},{7,8},{8,9},{9,10},{10,1... | collective-permute-start | bytes 786440 | tf_op jit(solution)/shard_map/ppermute | solution.py:20
  95.1 9.5 %collective-permute-start.11 = (f32[1024,64]{0,1:T(8,128)S(1)}, f32[1024,64]{0,1:T(8,128)S(1)}, u32[]{:S(2)}, u32[]{:S(2)}) collective-permute-start(f32[1024,64]{0,1:T(8,128)S(1)} %collective-permute-done.10), channel_id=1, source_target_pairs={{1,0},{2,1},{3,2},{4,3},{5,4},{6,5},{7,6},{8,7},{9,8},{10,9},{11,1... | collective-permute-start | bytes 786440 | tf_op jit(solution)/shard_map/ppermute | solution.py:22
  102.7 1.9 copy-start.3
  102.7 9.6 %collective-permute-start.5 = (f32[1024,64]{0,1:T(8,128)S(1)}, f32[1024,64]{0,1:T(8,128)}, u32[]{:S(2)}, u32[]{:S(2)}) collective-permute-start(f32[1024,64]{0,1:T(8,128)S(1)} %collective-permute-done.4), channel_id=1, source_target_pairs={{0,1},{1,2},{2,3},{3,4},{4,5},{5,6},{6,7},{7,8},{8,9},{9,10},{10,1... | collective-permute-start | bytes 786440 | tf_op jit(solution)/shard_map/ppermute | solution.py:20
  104.6 9.6 %collective-permute-start.12 = (f32[1024,64]{0,1:T(8,128)S(1)}, f32[1024,64]{0,1:T(8,128)}, u32[]{:S(2)}, u32[]{:S(2)}) collective-permute-start(f32[1024,64]{0,1:T(8,128)S(1)} %collective-permute-done.11), channel_id=1, source_target_pairs={{1,0},{2,1},{3,2},{4,3},{5,4},{6,5},{7,6},{8,7},{9,8},{10,9},{11,1... | collective-permute-start | bytes 786440 | tf_op jit(solution)/shard_map/ppermute | solution.py:22
  112.2 9.8 %collective-permute-start.6 = (f32[1024,64]{0,1:T(8,128)}, f32[1024,64]{0,1:T(8,128)}, u32[]{:S(2)}, u32[]{:S(2)}) collective-permute-start(f32[1024,64]{0,1:T(8,128)} %collective-permute-done.5), channel_id=1, source_target_pairs={{0,1},{1,2},{2,3},{3,4},{4,5},{5,6},{6,7},{7,8},{8,9},{9,10},{10,1... | collective-permute-start | bytes 786440 | tf_op jit(solution)/shard_map/ppermute | solution.py:20
  114.2 272.5 %reduce-scatter.5.cloned.1.call-start = ((), (), s32[]{:S(2)}) async-start(), calls=%async_computation.5 | async-start | bytes 540672 | tf_op jit(solution)/shard_map/reduce_scatter | solution.py:68
  114.3 9.8 %collective-permute-start.13 = (f32[1024,64]{0,1:T(8,128)}, f32[1024,64]{0,1:T(8,128)}, u32[]{:S(2)}, u32[]{:S(2)}) collective-permute-start(f32[1024,64]{0,1:T(8,128)} %collective-permute-done.12), channel_id=1, source_target_pairs={{1,0},{2,1},{3,2},{4,3},{5,4},{6,5},{7,6},{8,7},{9,8},{10,9},{11,1... | collective-permute-start | bytes 786440 | tf_op jit(solution)/shard_map/ppermute | solution.py:22
  122.0 9.8 %collective-permute-start.7 = (f32[1024,64]{0,1:T(8,128)}, f32[1024,64]{0,1:T(8,128)}, u32[]{:S(2)}, u32[]{:S(2)}) collective-permute-start(f32[1024,64]{0,1:T(8,128)} %collective-permute-done.6), channel_id=1, source_target_pairs={{0,1},{1,2},{2,3},{3,4},{4,5},{5,6},{6,7},{7,8},{8,9},{9,10},{10,1... | collective-permute-start | bytes 786440 | tf_op jit(solution)/shard_map/ppermute | solution.py:20
  124.0 24.4 %collective-permute-start.14 = (f32[1024,64]{0,1:T(8,128)}, f32[1024,64]{0,1:T(8,128)S(1)}, u32[]{:S(2)}, u32[]{:S(2)}) collective-permute-start(f32[1024,64]{0,1:T(8,128)} %collective-permute-done.13), channel_id=1, source_target_pairs={{1,0},{2,1},{3,2},{4,3},{5,4},{6,5},{7,6},{8,7},{9,8},{10,9},{11,1... | collective-permute-start | bytes 786440 | tf_op jit(solution)/shard_map/ppermute | solution.py:22
  267.2 13.7 %copy-start.2 = (f32[8,128,128]{1,2,0:T(8,128)}, f32[8,128,128]{1,2,0:T(8,128)S(1)}, u32[]{:S(2)}) copy-start(f32[8,128,128]{1,2,0:T(8,128)S(1)} %custom-call.4) | copy-start | bytes 1572868
  267.3 5.1 %copy-start.1 = (f32[512,1024]{0,1:T(8,128)S(1)}, f32[512,1024]{0,1:T(8,128)}, u32[]{:S(2)}) copy-start(f32[512,1024]{0,1:T(8,128)} %all-gather.3.cloned.1.call-done) | copy-start | bytes 6291460
  283.7 1.5 copy-start.4
  287.8 204.6 %reduce-scatter.3.cloned.1.call-start = ((), (), s32[]{:S(2)}) async-start(), calls=%async_computation.4 | async-start | bytes 2162688 | tf_op jit(solution)/shard_map/reduce_scatter | solution.py:61
  293.6 93.1 %copy-start.6 = (f32[32,64]{1,0:T(8,128)S(1)}, f32[32,64]{1,0:T(8,128)}, u32[]{:S(2)}) copy-start(f32[32,64]{1,0:T(8,128)} %param.15) | copy-start | bytes 24580
  293.6 198.8 %copy-start.5 = (f32[32,512]{1,0:T(8,128)S(1)}, f32[32,512]{1,0:T(8,128)}, u32[]{:S(2)}) copy-start(f32[32,512]{1,0:T(8,128)} %param.14) | copy-start | bytes 196612
Sparse Core Ops, SparseCore 0:
  10.1 80.8 all-gather.2
  114.3 58.1 all-gather.4
  287.9 98.7 reduce-scatter.4
  391.0 101.3 reduce-scatter.2
